TPU v7x, 32 devices: a whole 2x2x4 slice. The times are simulated.
32 devices in a mesh: frame: 4 (over y, core), tensor: 8 (over z, x).
Axes of the slice: x: 2, y: 2, z: 4, core: 2. Of those that a mesh axis runs over, the one named last changes fastest.
Arguments:
- latent: bfloat16 [7680, 1152], P('frame', 'tensor'), may hold values from -6 to 6
- timestep: int32 [1], replicated, may hold values from 0 to 999
- frame_pos: int32 [4], P('frame'), may hold values from 0 to 4095
- time_w1: bfloat16 [256, 1152], replicated, may hold values from -0.375 to 0.375
- time_w2: bfloat16 [1152, 1152], P(None, 'tensor'), may hold values from -0.1875 to 0.1875
- ada_w: bfloat16 [1152, 10368], P('tensor'), may hold values from -0.1875 to 0.1875
- w_sqkv: bfloat16 [1152, 3456], P(None, 'tensor'), may hold values from -0.70710678 to 0.70710678
- w_so: bfloat16 [1152, 1152], P('tensor'), may hold values from -0.25 to 0.25
- w_tqkv: bfloat16 [1152, 3456], P(None, 'tensor'), may hold values from -0.70710678 to 0.70710678
- w_to: bfloat16 [1152, 1152], P('tensor'), may hold values from -0.25 to 0.25
- w_fc1: bfloat16 [1152, 4608], P(None, 'tensor'), may hold values from -0.1875 to 0.1875
- w_fc2: bfloat16 [4608, 1152], P('tensor'), may hold values from -0.125 to 0.125
Outputs:
- block_out: bfloat16 [7680, 1152], P('frame', 'tensor')
All inputs are finite; a program needn't handle non-finite values.
Results may differ from a plain program's by a relative error of at most 0.025.
Values may be sent and summed in bfloat16 or wider, within the bound.
A program may use at most 128 MiB of HBM per device.

v0:
```python
import math

import jax
import jax.numpy as jnp
from jax import lax
from jax.experimental import pallas as pl
from jax.experimental.pallas import tpu as pltpu
from jax.sharding import PartitionSpec as P

D = 1152
HD = 72
P_SIZE = 1920


def layer_norm(values_in):
    center = values_in - jnp.mean(values_in, axis=-1, keepdims=True)
    spread = jnp.mean(center * center, axis=-1, keepdims=True)
    return center * lax.rsqrt(spread + 1e-06)


def branch_input(stream, shift, scale):
    return (layer_norm(stream.astype(jnp.float32)) * (1.0 + scale) + shift).astype(jnp.bfloat16)


def time_features(timestep, width):
    half_width = width // 2
    frequency = jnp.exp(-math.log(10000.0) * jnp.arange(half_width, dtype=jnp.float32) / half_width)
    angles = timestep.astype(jnp.float32)[:, None] * frequency[None, :]
    return jnp.concatenate([jnp.cos(angles), jnp.sin(angles)], axis=1).astype(jnp.bfloat16)


def bdot(a, b):
    return jnp.dot(a, b, preferred_element_type=jnp.float32)


def ring_place(index, n):
    odd = index % 2
    return (1 - odd) * (index // 2) + odd * (n - 1 - index // 2)


def ring_member(place, n):
    back = place // (n // 2)
    return (1 - back) * (2 * place) + back * (2 * (n - 1 - place) + 1)


def exchange_kernel(n, x_ref, part_ref, full_ref, mods_ref, send, recv, msend, mrecv, local):
    me = lax.axis_index("tensor")
    place = ring_place(me, n)
    rows = x_ref.shape[0]
    half = n // 2
    cut = max(16, -(-rows // 32) * 16)

    def member(offset):
        return ring_member(lax.rem(place + offset + 2 * n, n), n)

    barrier = pltpu.get_barrier_semaphore()
    for k in range(1, n):
        peer = lax.rem(me + k, n)
        pl.semaphore_signal(
            barrier, inc=1, device_id={"tensor": peer}, device_id_type=pl.DeviceIdType.MESH
        )
    pl.semaphore_wait(barrier, n - 1)

    def hop(direction, step, lo, size, owner):
        source = x_ref if step == 0 else full_ref.at[owner]
        return pltpu.make_async_remote_copy(
            src_ref=source.at[pl.ds(lo, size)],
            dst_ref=full_ref.at[owner, pl.ds(lo, size)],
            send_sem=send.at[direction, step],
            recv_sem=recv.at[direction, step],
            device_id={"tensor": member(1 if direction == 0 else -1)},
            device_id_type=pl.DeviceIdType.MESH,
        )

    def span(direction, step):
        if step < half - 1:
            return 0, rows
        return (0, cut) if direction == 0 else (cut, rows - cut)

    def outgoing(direction, step):
        lo, size = span(direction, step)
        return hop(direction, step, lo, size, member(-step if direction == 0 else step))

    def incoming(direction, step):
        lo, size = span(direction, step)
        sign = -1 if direction == 0 else 1
        return hop(direction, step, lo, size, member(sign * (step + 1)))

    def mod_copy(slot, peer):
        return pltpu.make_async_remote_copy(
            src_ref=part_ref,
            dst_ref=mods_ref.at[slot],
            send_sem=msend.at[peer],
            recv_sem=mrecv.at[slot],
            device_id={"tensor": peer},
            device_id_type=pl.DeviceIdType.MESH,
        )

    own = pltpu.make_async_copy(x_ref, full_ref.at[me], local)
    mods_ref[me] = part_ref[...]
    for direction in range(2):
        outgoing(direction, 0).start()
    for k in range(1, n):
        mod_copy(me, lax.rem(me + k, n)).start()
    own.start()
    for step in range(1, half):
        for direction in range(2):
            incoming(direction, step - 1).wait_recv()
            outgoing(direction, step).start()
    for direction in range(2):
        incoming(direction, half - 1).wait_recv()
    for step in range(half):
        for direction in range(2):
            outgoing(direction, step).wait_send()
    for k in range(1, n):
        peer = lax.rem(me + k, n)
        mod_copy(peer, peer).wait_recv()
        mod_copy(me, peer).wait_send()
    own.wait()


def exchange(n, x_block, part):
    half = n // 2
    vmem = pl.BlockSpec(memory_space=pltpu.VMEM)
    return pl.pallas_call(
        lambda *refs: exchange_kernel(n, *refs),
        out_shape=(
            jax.ShapeDtypeStruct((n,) + x_block.shape, x_block.dtype),
            jax.ShapeDtypeStruct((n,) + part.shape, part.dtype),
        ),
        in_specs=[vmem, vmem],
        out_specs=(vmem, vmem),
        scratch_shapes=[
            pltpu.SemaphoreType.DMA((2, half)),
            pltpu.SemaphoreType.DMA((2, half)),
            pltpu.SemaphoreType.DMA((n,)),
            pltpu.SemaphoreType.DMA((n,)),
            pltpu.SemaphoreType.DMA,
        ],
        compiler_params=pltpu.CompilerParams(
            collective_id=0, has_side_effects=True, vmem_limit_bytes=24 * 1024 * 1024
        ),
        cost_estimate=pl.CostEstimate(flops=0, bytes_accessed=100_000_000, transcendentals=0),
        name="exchange",
    )(x_block, part)


def spatial_attention(normed_t, w_qkv):
    heads_local = w_qkv.shape[1] // (3 * HD)
    projected = jnp.einsum(
        "kn,kp->np", w_qkv, normed_t, preferred_element_type=jnp.float32
    ).astype(jnp.bfloat16)
    projected = projected.reshape(heads_local, 3, HD, P_SIZE)
    scores = jnp.einsum(
        "hdp,hdq->hpq", projected[:, 0], projected[:, 1], preferred_element_type=jnp.float32
    ) * HD ** (-0.5)
    weights = jax.nn.softmax(scores, axis=-1).astype(jnp.bfloat16)
    attended = jnp.einsum(
        "hpq,hdq->phd", weights, projected[:, 2], preferred_element_type=jnp.float32
    ).astype(jnp.bfloat16)
    return attended.reshape(P_SIZE, heads_local * HD)


HALF = HD // 2
SLOT = -(-HALF // 16) * 16


def padded_halves(rows):
    split = rows.reshape((-1, HALF) + rows.shape[1:])
    return jnp.pad(split, ((0, 0), (0, SLOT - HALF)) + ((0, 0),) * (rows.ndim - 1))


def gather_units(units, frame_count, frame_index):
    if units.shape[0] % frame_count:
        full = lax.all_gather(units, "tensor", axis=0, tiled=True)
        return full
    part = units.shape[0] // frame_count
    mine = lax.dynamic_slice_in_dim(units, frame_index * part, part, 0)
    return lax.all_gather(mine, ("tensor", "frame"), axis=0, tiled=True)


def joined_half(core, first, second):
    half = first.shape[0] // 2
    return jnp.concatenate(
        [lax.dynamic_slice_in_dim(w, core * half, half, 0) for w in (first, second)], axis=0
    )


def ring_blocks(n, block):
    order = [ring_member(place, n) for place in range(n)]
    right = [(order[p], order[(p + 1) % n]) for p in range(n)]
    left = [(b, a) for a, b in right]
    blocks = [block]
    from_left, from_right = block, block
    for step in range(n // 2):
        from_left = lax.ppermute(from_left, "tensor", right)
        blocks.append(from_left)
        if step < n // 2 - 1:
            from_right = lax.ppermute(from_right, "tensor", left)
            blocks.append(from_right)
    return blocks


def temporal_kernel(frames, q_ref, k_ref, v_ref, cos_ref, sin_ref, o_ref):
    rows, width = q_ref.shape
    pp = rows // frames
    lane = lax.broadcasted_iota(jnp.int32, (pp, width), 1)
    first = lane % (2 * SLOT) < SLOT
    gather = (
        lax.broadcasted_iota(jnp.int32, (width, 128), 0) // (2 * SLOT)
        == lax.broadcasted_iota(jnp.int32, (width, 128), 1)
    ).astype(jnp.bfloat16)
    spread = (
        lax.broadcasted_iota(jnp.int32, (128, width), 1) // (2 * SLOT)
        == lax.broadcasted_iota(jnp.int32, (128, width), 0)
    ).astype(jnp.bfloat16)

    def turned(ref, f):
        x = ref[f * pp : (f + 1) * pp, :].astype(jnp.float32)
        partner = jnp.where(
            first, pltpu.roll(x, width - SLOT, axis=1), pltpu.roll(x, SLOT, axis=1)
        )
        x = x * cos_ref[f : f + 1, :] + partner * sin_ref[f : f + 1, :]
        return x.astype(jnp.bfloat16).astype(jnp.float32)

    keys = [turned(k_ref, f) for f in range(frames)]
    for f in range(frames):
        query = turned(q_ref, f)
        product = jnp.concatenate([query * key for key in keys], axis=0)
        high = product.astype(jnp.bfloat16)
        low = (product - high.astype(jnp.float32)).astype(jnp.bfloat16)
        scores = (bdot(high, gather) + bdot(low, gather)) * HD ** (-0.5)
        parts = [scores[g * pp : (g + 1) * pp] for g in range(frames)]
        top = parts[0]
        for part in parts[1:]:
            top = jnp.maximum(top, part)
        parts = [jnp.exp(part - top) for part in parts]
        total = parts[0]
        for part in parts[1:]:
            total = total + part
        weights = [(part / total).astype(jnp.bfloat16) for part in parts]
        wide = bdot(jnp.concatenate(weights, axis=0), spread)
        out = jnp.zeros((pp, width), jnp.float32)
        for g in range(frames):
            rows_g = slice(g * pp, (g + 1) * pp)
            out = out + wide[rows_g] * v_ref[rows_g, :].astype(jnp.float32)
        o_ref[f * pp : (f + 1) * pp, :] = out.astype(jnp.bfloat16)


def temporal_attention(q, k, v, frame_pos):
    frames = frame_pos.shape[0]
    frequency = jnp.exp(-math.log(10000.0) * jnp.arange(HALF, dtype=jnp.float32) / HALF)
    angles = frame_pos.astype(jnp.float32)[:, None] * frequency[None, :]
    fill = ((0, 0), (0, SLOT - HALF))
    cosine = jnp.pad(jnp.cos(angles), fill)
    sine = jnp.pad(jnp.sin(angles), fill)
    slots = q.shape[1] // SLOT
    cosine = jnp.tile(cosine, (1, slots))
    sine = jnp.tile(jnp.concatenate([-sine, sine], axis=1), (1, slots // 2))
    vmem = pl.BlockSpec(memory_space=pltpu.VMEM)
    return pl.pallas_call(
        lambda *refs: temporal_kernel(frames, *refs),
        out_shape=jax.ShapeDtypeStruct(q.shape, q.dtype),
        in_specs=[vmem] * 5,
        out_specs=vmem,
        compiler_params=pltpu.CompilerParams(vmem_limit_bytes=32 * 1024 * 1024),
        name="temporal",
    )(q, k, v, cosine, sine)


def shards(
    latent, timestep, frame_pos, time_w1, time_w2, ada_w, w_sqkv, w_so, w_tqkv, w_to, w_fc1, w_fc2
):
    frames = lax.axis_size("frame")
    tensors = lax.axis_size("tensor")
    count = frames * tensors
    frame_index = lax.axis_index("frame")
    width = latent.shape[1]
    pp = -(-P_SIZE // (count * 16)) * 16
    padded = count * pp

    time_embed = time_features(timestep, time_w1.shape[0])
    hidden_time = jax.nn.silu(bdot(time_embed, time_w1)).astype(jnp.bfloat16)
    condition = jax.nn.silu(bdot(hidden_time, time_w2)).astype(jnp.bfloat16)
    partial_mod = bdot(condition, ada_w).reshape(-1, 128)
    part_rows = partial_mod.shape[0]
    partial_mod = jnp.pad(partial_mod, ((0, -part_rows % 8), (0, 0)))

    qkv_units = w_tqkv.T.reshape(-1, 3, 2, HALF, D).transpose(0, 2, 1, 3, 4)
    qkv_units = jnp.pad(qkv_units, ((0, 0),) * 3 + ((0, SLOT - HALF), (0, 0)))
    units = jnp.concatenate(
        [qkv_units.reshape(-1, 3 * SLOT, D), padded_halves(w_so), padded_halves(w_to)], axis=1
    )
    gathered = gather_units(units, frames, frame_index)
    wq, wk, wv, full_so, full_to = (
        gathered[:, i * SLOT : (i + 1) * SLOT].reshape(-1, D) for i in range(5)
    )
    all_pos = lax.all_gather(frame_pos, "frame", axis=0, tiled=True)

    full_t, mods = exchange(tensors, latent.T, partial_mod)
    full_t = full_t.reshape(D, P_SIZE)
    modulation = jnp.sum(mods, axis=0)[:part_rows].reshape(-1)
    full_t, w_fc1, w_fc2 = lax.optimization_barrier((full_t, w_fc1, w_fc2))
    mlp_blocks = ring_blocks(tensors, joined_half(frame_index % 2, w_fc1.T, w_fc2))

    def mod_vector(index):
        return modulation[index * D : (index + 1) * D]

    def to_patches(block):
        own = block.shape[1]
        block = jnp.pad(block, ((0, padded - P_SIZE), (0, 0))).reshape(count, pp, own)
        got = lax.all_to_all(block, ("frame", "tensor"), 0, 0, tiled=True)
        return got.reshape(frames, tensors, pp, own).transpose(0, 2, 1, 3)

    def to_features(rows):
        block = rows.reshape(frames, pp, tensors, width).transpose(0, 2, 1, 3)
        got = lax.all_to_all(
            block.reshape(count, pp, width), ("frame", "tensor"), 0, 0, tiled=True
        )
        return got.reshape(padded, width)[:P_SIZE]

    rows_t = full_t.astype(jnp.float32)
    center = rows_t - jnp.mean(rows_t, axis=0, keepdims=True)
    spread = jnp.mean(center * center, axis=0, keepdims=True)
    normed_t = center * lax.rsqrt(spread + 1e-06)
    normed_t = normed_t * (1.0 + mod_vector(1))[:, None] + mod_vector(0)[:, None]
    attended = spatial_attention(normed_t.astype(jnp.bfloat16), w_sqkv)
    attended = jnp.pad(
        attended.reshape(P_SIZE, -1, HALF), ((0, 0), (0, 0), (0, SLOT - HALF))
    ).reshape(P_SIZE, -1)
    slot_width = attended.shape[1]
    arrived = to_patches(jnp.concatenate([attended, latent], axis=1))
    attended = arrived[..., :slot_width].reshape(frames * pp, -1)
    residual = arrived[..., slot_width:].reshape(frames * pp, D).astype(jnp.float32)

    def rows_by(a, w):
        return jnp.einsum("rk,nk->rn", a, w, preferred_element_type=jnp.float32)

    stream = (residual + mod_vector(2) * bdot(attended, full_so)).astype(jnp.bfloat16)
    normed = branch_input(stream, mod_vector(3), mod_vector(4))
    q, k, v = (rows_by(normed, w).astype(jnp.bfloat16) for w in (wq, wk, wv))
    attended = temporal_attention(q, k, v, all_pos)
    stream = (stream.astype(jnp.float32) + mod_vector(5) * bdot(attended, full_to)).astype(
        jnp.bfloat16
    )
    normed = branch_input(stream, mod_vector(6), mod_vector(7))
    swap = [(i, i ^ 1) for i in range(frames)]
    both = jnp.concatenate([normed, lax.ppermute(normed, "frame", swap)], axis=0)
    half = mlp_blocks[0].shape[0] // 2
    first = jnp.concatenate([block[:half] for block in mlp_blocks], axis=0)
    second = jnp.concatenate([block[half:] for block in mlp_blocks], axis=0)
    hidden = jax.nn.gelu(rows_by(both, first), approximate=True).astype(jnp.bfloat16)
    total = bdot(hidden, second)
    count_rows = normed.shape[0]
    other = lax.ppermute(total[count_rows:].astype(jnp.bfloat16), "frame", swap)
    summed = total[:count_rows] + other.astype(jnp.float32)
    out = stream.astype(jnp.float32) + mod_vector(8) * summed
    return to_features(out.astype(jnp.bfloat16))


def solution(mesh):
    placed = (
        P("frame", "tensor"),
        P(),
        P("frame"),
        P(),
        P(None, "tensor"),
        P("tensor", None),
        P(None, "tensor"),
        P("tensor", None),
        P(None, "tensor"),
        P("tensor", None),
        P(None, "tensor"),
        P("tensor", None),
    )
    return jax.shard_map(
        shards, mesh=mesh, in_specs=placed, out_specs=P("frame", "tensor"), check_vma=False
    )
```

profile of v0, /device:TPU:0, one launch (start us, length us, event | category | flops | bytes accessed | tf_op | source)
XLA Modules:
  0.0 377.8 jit_solution(4547547908951953678)
XLA Ops:
  20.1 91.7 %exchange.1 = (bf16[8,144,1920]{2,1,0:T(8,128)(2,1)S(1)}, f32[8,88,128]{2,1,0:T(8,128)S(1)}) custom-call(bf16[144,1920]{1,0:T(8,128)(2,1)S(1)} %bitcast.114, f32[88,128]{1,0:T(8,128)S(1)} %pad.30.refs_1_), custom_call_target="tpu_custom_call" | custom-call | bytes 100000000 | tf_op jit(solution)/shard_map/exchange/pallas_call | solution.py:125
  121.9 3.1 convert_reduce_fusion
  126.8 4.0 %fusion.33 = bf16[1920,432]{0,1:T(8,128)(2,1)} fusion(bf16[1152,432]{0,1:T(8,128)(2,1)S(1)} %copy-done.7, bf16[1152,1920]{1,0:T(8,128)(2,1)S(1)} %bitcast.113, f32[1152]{0:T(1024)S(1)} %get-tuple-element.45, f32[1152]{0:T(1024)S(1)} %get-tuple-element.46, f32[1920]{0:T(1024)S(1)} %add_rsqrt_fusion, f32[1920]{0:T(1024)S(1)} %broadcast_multiply_fusion), kind=kOutput, calls=%fused_computation.36 | convolution fusion | flops 1925130240 | bytes 7102464 | tf_op jit(solution)/shard_map/kn,kp->np/dot_general | solution.py:150
  130.8 15.1 %fusion.80 = (f32[2,1920]{1,0:T(2,128)S(1)}, f32[2,1920,1920]{1,2,0:T(8,128)}) fusion(bf16[2,3,72,1920]{3,2,1,0:T(8,128)(2,1)} %bitcast.131), kind=kOutput, calls=%fused_computation.143 | convolution fusion | flops 1083803520 | bytes 30612480 | tf_op jit(solution)/shard_map/sub | solution.py:157
  145.9 12.1 %fusion.49 = bf16[1920,2,72]{0,2,1:T(8,128)(2,1)S(1)} fusion(f32[2,1920,1920]{1,2,0:T(8,128)} %get-tuple-element.52, f32[2,1920]{1,0:T(2,128)S(1)} %get-tuple-element.51, bf16[2,3,72,1920]{3,2,1,0:T(8,128)(2,1)} %bitcast.132), kind=kOutput, calls=%fused_computation.54 | convolution fusion | flops 1076705280 | bytes 30612480 | tf_op jit(solution)/shard_map/hpq,hdq->phd/dot_general | solution.py:158
  163.4 4.0 %all-to-all-start = ((bf16[32,64,336]{2,1,0:T(8,128)(2,1)}), bf16[32,64,336]{2,1,0:T(8,128)(2,1)S(1)}, u32[]{:S(2)}, u32[]{:S(2)}) async-start(bf16[32,64,336]{2,1,0:T(8,128)(2,1)} %bitcast.117), calls=%async_computation | async-start | bytes 3145728 | tf_op jit(solution)/shard_map/all_to_all | solution.py:312
  167.5 5.2 %all-reduce.8 = s32[4]{0:T(128)S(1)} all-reduce(s32[4]{0:T(128)S(1)} %dynamic-update-slice), channel_id=1, replica_groups=mesh['frame'=4,'tensor'=8] {'frame'}, use_global_device_ids=true, to_apply=%add.8 | all-reduce | flops 4 | bytes 32
  172.7 4.3 %collective-permute-done.1 = bf16[576,1152]{1,0:T(8,128)(2,1)} collective-permute-done((bf16[576,1152]{1,0:T(8,128)(2,1)}, bf16[576,1152]{1,0:T(8,128)(2,1)}, u32[]{:S(2)}, u32[]{:S(2)}) %collective-permute-start.1) | collective-permute-done | bytes 1327136 | tf_op jit(solution)/shard_map/ppermute | solution.py:196
  177.0 21.4 %collective-permute-start.3 = (bf16[576,1152]{1,0:T(8,128)(2,1)}, bf16[576,1152]{1,0:T(8,128)(2,1)}, u32[]{:S(2)}, u32[]{:S(2)}) collective-permute-start(bf16[576,1152]{1,0:T(8,128)(2,1)} %collective-permute-done.1), channel_id=1, source_target_pairs={{0,2},{2,4},{4,6},{6,7},{7,5},{5,3},{3,1},{1,0},{8,10},{10,12},{12... | collective-permute-start | bytes 3981320 | tf_op jit(solution)/shard_map/ppermute | solution.py:196
  201.2 2.5 slice_dynamic-update-slice_fusion.12
  203.7 39.7 %collective-permute-done.3 = bf16[576,1152]{1,0:T(8,128)(2,1)} collective-permute-done((bf16[576,1152]{1,0:T(8,128)(2,1)}, bf16[576,1152]{1,0:T(8,128)(2,1)}, u32[]{:S(2)}, u32[]{:S(2)}) %collective-permute-start.3) | collective-permute-done | bytes 1327136 | tf_op jit(solution)/shard_map/ppermute | solution.py:196
  243.4 9.9 %collective-permute-start.5 = (bf16[576,1152]{1,0:T(8,128)(2,1)}, bf16[576,1152]{1,0:T(8,128)(2,1)}, u32[]{:S(2)}, u32[]{:S(2)}) collective-permute-start(bf16[576,1152]{1,0:T(8,128)(2,1)} %collective-permute-done.3), channel_id=1, source_target_pairs={{0,2},{2,4},{4,6},{6,7},{7,5},{5,3},{3,1},{1,0},{8,10},{10,12},{12... | collective-permute-start | bytes 3981320 | tf_op jit(solution)/shard_map/ppermute | solution.py:196
  253.3 2.5 slice_dynamic-update-slice_fusion.11
  255.8 2.5 slice_dynamic-update-slice_fusion.10
  265.7 15.9 %collective-permute-done.5 = bf16[576,1152]{1,0:T(8,128)(2,1)} collective-permute-done((bf16[576,1152]{1,0:T(8,128)(2,1)}, bf16[576,1152]{1,0:T(8,128)(2,1)}, u32[]{:S(2)}, u32[]{:S(2)}) %collective-permute-start.5) | collective-permute-done | bytes 1327136 | tf_op jit(solution)/shard_map/ppermute | solution.py:196
  281.6 2.5 collective-permute-start.7
  284.1 2.5 slice_dynamic-update-slice_fusion.9
  286.5 9.0 %fusion.79 = (bf16[32,48,1152]{2,1,0:T(8,128)(2,1)S(1)}, bf16[32,48,1152]{2,1,0:T(8,128)(2,1)S(1)}, bf16[32,48,1152]{2,1,0:T(8,128)(2,1)S(1)}, bf16[32,48,1152]{2,1,0:T(8,128)(2,1)S(1)}, bf16[32,48,1152]{2,1,0:T(8,128)(2,1)}) fusion(bf16[32,240,1152]{2,1,0:T(8,128)(2,1)} %all-gather.2.cloned.1.call-done), kind=kLoop, calls=%fused_computation.142 | loop fusion | bytes 35389440 | tf_op jit(solution)/shard_map/slice | solution.py:296
  295.5 3.3 fusion.81
  303.1 5.1 %temporal.1 = bf16[256,1536]{1,0:T(8,128)(2,1)S(1)} custom-call(bf16[256,1536]{1,0:T(8,128)(2,1)S(1)} %convolution_convert_fusion.2.refs_0_, bf16[256,1536]{1,0:T(8,128)(2,1)S(1)} %convolution_convert_fusion.1.refs_1_, bf16[256,1536]{1,0:T(8,128)(2,1)S(1)} %convolution_convert_fusion.refs_2_, f32[4,1536]{1,0:T(4,128)S(1)} %tile.9.refs_3_, ...), custom_call_target="tpu_custom_call" | custom-call | tf_op jit(solution)/shard_map/temporal/pallas_call | solution.py:261
  310.2 2.5 slice_dynamic-update-slice_fusion.8
  314.8 2.5 slice_dynamic-update-slice_fusion.7
  317.3 12.3 %fusion.43 = f32[512,1152]{1,0:T(8,128)} fusion(bf16[2304,1152]{1,0:T(8,128)(2,1)} %get-tuple-element.25, bf16[2304,1152]{1,0:T(8,128)(2,1)} %get-tuple-element.24, bf16[256,1152]{1,0:T(8,128)(2,1)S(1)} %collective-permute-done, bf16[256,1152]{1,0:T(8,128)(2,1)S(1)} %add_convert_fusion), kind=kOutput, calls=%fused_computation.49 | convolution fusion | flops 5448794112 | bytes 14155776 | tf_op jit(solution)/shard_map/dot_general | solution.py:33
  336.0 31.4 %all_to_all.10 = bf16[32,64,144]{2,1,0:T(8,128)(2,1)S(1)} all-to-all(bf16[32,64,144]{2,1,0:T(8,128)(2,1)S(1)} %bitcast.120), channel_id=1, replica_groups=mesh['frame'=4,'tensor'=8] {'frame','tensor'}, dimensions={0} | all-to-all | bytes 1179648 | tf_op jit(solution)/shard_map/all_to_all | solution.py:317
  (102 shorter events, 57.7 us)
Async XLA Ops:
  6.5 13.1 %copy-start = (bf16[144,10368]{1,0:T(8,128)(2,1)S(1)}, bf16[144,10368]{1,0:T(8,128)(2,1)}, u32[]{:S(2)}) copy-start(bf16[144,10368]{1,0:T(8,128)(2,1)} %param.17) | copy-start | bytes 8957956
  6.5 280.0 %all-gather.2.cloned.1.call-start = ((), (), s32[]{:S(2)}) async-start(), calls=%async_computation.2 | async-start | bytes 18247680 | tf_op jit(solution)/shard_map/all_gather | solution.py:179
  14.0 1.4 copy-start.5
  16.2 3.9 %copy-start.4 = (bf16[1920,144]{0,1:T(8,128)(2,1)S(1)}, bf16[1920,144]{0,1:T(8,128)(2,1)}, u32[]{:S(2)}) copy-start(bf16[1920,144]{0,1:T(8,128)(2,1)} %param.12) | copy-start | bytes 1658884
  111.8 2.0 copy-start.2
  119.4 57.6 %collective-permute-start.1 = (bf16[576,1152]{1,0:T(8,128)(2,1)}, bf16[576,1152]{1,0:T(8,128)(2,1)}, u32[]{:S(2)}, u32[]{:S(2)}) collective-permute-start(bf16[576,1152]{1,0:T(8,128)(2,1)} %pad_maximum_fusion), channel_id=1, source_target_pairs={{0,2},{2,4},{4,6},{6,7},{7,5},{5,3},{3,1},{1,0},{8,10},{10,12},{12... | collective-permute-start | bytes 3981320 | tf_op jit(solution)/shard_map/ppermute | solution.py:196
  120.5 77.8 %collective-permute-start.2 = (bf16[576,1152]{1,0:T(8,128)(2,1)}, bf16[576,1152]{1,0:T(8,128)(2,1)}, u32[]{:S(2)}, u32[]{:S(2)}) collective-permute-start(bf16[576,1152]{1,0:T(8,128)(2,1)} %pad_maximum_fusion), channel_id=1, source_target_pairs={{2,0},{4,2},{6,4},{7,6},{5,7},{3,5},{1,3},{0,1},{10,8},{12,10},{14... | collective-permute-start | bytes 3981320 | tf_op jit(solution)/shard_map/ppermute | solution.py:199
  121.9 3.6 copy-start.3
  125.0 1.7 copy-start.7
  158.0 2.1 copy-start.8
  163.4 94.9 %all-to-all-start = ((bf16[32,64,336]{2,1,0:T(8,128)(2,1)}), bf16[32,64,336]{2,1,0:T(8,128)(2,1)S(1)}, u32[]{:S(2)}, u32[]{:S(2)}) async-start(bf16[32,64,336]{2,1,0:T(8,128)(2,1)} %bitcast.117), calls=%async_computation | async-start | bytes 3145728 | tf_op jit(solution)/shard_map/all_to_all | solution.py:312
  177.0 66.4 %collective-permute-start.3 = (bf16[576,1152]{1,0:T(8,128)(2,1)}, bf16[576,1152]{1,0:T(8,128)(2,1)}, u32[]{:S(2)}, u32[]{:S(2)}) collective-permute-start(bf16[576,1152]{1,0:T(8,128)(2,1)} %collective-permute-done.1), channel_id=1, source_target_pairs={{0,2},{2,4},{4,6},{6,7},{7,5},{5,3},{3,1},{1,0},{8,10},{10,12},{12... | collective-permute-start | bytes 3981320 | tf_op jit(solution)/shard_map/ppermute | solution.py:196
  198.4 54.9 %collective-permute-start.4 = (bf16[576,1152]{1,0:T(8,128)(2,1)}, bf16[576,1152]{1,0:T(8,128)(2,1)}, u32[]{:S(2)}, u32[]{:S(2)}) collective-permute-start(bf16[576,1152]{1,0:T(8,128)(2,1)} %collective-permute-done.2), channel_id=1, source_target_pairs={{2,0},{4,2},{6,4},{7,6},{5,7},{3,5},{1,3},{0,1},{10,8},{12,10},{14... | collective-permute-start | bytes 3981320 | tf_op jit(solution)/shard_map/ppermute | solution.py:199
  243.4 38.2 %collective-permute-start.5 = (bf16[576,1152]{1,0:T(8,128)(2,1)}, bf16[576,1152]{1,0:T(8,128)(2,1)}, u32[]{:S(2)}, u32[]{:S(2)}) collective-permute-start(bf16[576,1152]{1,0:T(8,128)(2,1)} %collective-permute-done.3), channel_id=1, source_target_pairs={{0,2},{2,4},{4,6},{6,7},{7,5},{5,3},{3,1},{1,0},{8,10},{10,12},{12... | collective-permute-start | bytes 3981320 | tf_op jit(solution)/shard_map/ppermute | solution.py:196
  253.3 56.9 %collective-permute-start.6 = (bf16[576,1152]{1,0:T(8,128)(2,1)}, bf16[576,1152]{1,0:T(8,128)(2,1)}, u32[]{:S(2)}, u32[]{:S(2)}) collective-permute-start(bf16[576,1152]{1,0:T(8,128)(2,1)} %collective-permute-done.4), channel_id=1, source_target_pairs={{2,0},{4,2},{6,4},{7,6},{5,7},{3,5},{1,3},{0,1},{10,8},{12,10},{14... | collective-permute-start | bytes 3981320 | tf_op jit(solution)/shard_map/ppermute | solution.py:199
  281.6 33.3 %collective-permute-start.7 = (bf16[576,1152]{1,0:T(8,128)(2,1)}, bf16[576,1152]{1,0:T(8,128)(2,1)}, u32[]{:S(2)}, u32[]{:S(2)}) collective-permute-start(bf16[576,1152]{1,0:T(8,128)(2,1)} %collective-permute-done.5), channel_id=1, source_target_pairs={{0,2},{2,4},{4,6},{6,7},{7,5},{5,3},{3,1},{1,0},{8,10},{10,12},{12... | collective-permute-start | bytes 3981320 | tf_op jit(solution)/shard_map/ppermute | solution.py:196
  286.5 9.0 %copy-start.6 = (f32[256,1152]{1,0:T(8,128)S(1)}, f32[256,1152]{1,0:T(8,128)}, u32[]{:S(2)}) copy-start(f32[256,1152]{1,0:T(8,128)} %reshape.208) | copy-start | bytes 3538948
  310.1 7.2 %collective-permute-start = (bf16[256,1152]{1,0:T(8,128)(2,1)S(1)}, bf16[256,1152]{1,0:T(8,128)(2,1)S(1)}, u32[]{:S(2)}, u32[]{:S(2)}) collective-permute-start(bf16[256,1152]{1,0:T(8,128)(2,1)S(1)} %add_convert_fusion), channel_id=1, source_target_pairs={{0,8},{8,0},{16,24},{24,16},{1,9},{9,1},{17,25},{25,17},{2,10},{10... | collective-permute-start | bytes 1769480 | tf_op jit(solution)/shard_map/ppermute | solution.py:348
  330.9 2.1 collective-permute-start.8
  336.0 34.7 %copy-start.1 = (bf16[144,10368]{1,0:T(8,128)(2,1)S(1)}, bf16[144,10368]{1,0:T(8,128)(2,1)}, u32[]{:S(2)}) copy-start(bf16[144,10368]{1,0:T(8,128)(2,1)} %param.17) | copy-start | bytes 8957956
Sparse Core Ops, SparseCore 0:
  16.4 190.3 all-gather.1
where the time goes:
time: 381 us; the launch traced here: 378 us
  Pallas kernels  96.8 us (25%)
  waiting for transfers between devices  64.1 us (17%)
  local copies, waits for them, and re-layouts  58.4 us (15%)
  matrix products  55 us (14%)
  starting transfers between devices  40.5 us (11%)
  blocking collectives  36.6 us (10%)
  between operations  15.4 us (4%)
  other arithmetic  11.1 us (3%)
    pallas_call x1, Pallas kernels, exchange(): pl.pallas_call(lambda *refs: exchange_kernel(n, *refs), out_shape=(jax.Sh...  91.7 us
    ppermute x4, waiting for transfers between devices, ring_blocks(): from_left = lax.ppermute(from_left, 'tensor', right)  62 us
    ppermute x4, starting transfers between devices, ring_blocks(): from_left = lax.ppermute(from_left, 'tensor', right)  34.9 us
    all_to_all x1, blocking collectives, to_features(): lax.all_to_all(block.reshape(count, pp, width), ('frame', 'tensor'), 0, 0...  31.4 us
    unnamed x31, local copies, waits for them, and re-layouts  26 us
    dot_general x6, matrix products, bdot(): return jnp.dot(a, b, preferred_element_type=jnp.float32)  19.7 us
    sub x1, matrix products, spatial_attention(): weights = jax.nn.softmax(scores, axis=-1).astype(jnp.bfloat16)  15.1 us
    dot_general x1, matrix products, spatial_attention(): jnp.einsum('hpq,hdq->phd', weights, projected[:, 2], preferred_element_ty...  12.1 us
  transfers between devices with their start and end apart: 11, of which 5 were waited for; matrix products, arithmetic and copies ran while one was open for 24% of the time, Pallas kernels for 26%

commit v1 on v0

--- a/solution.py
+++ b/solution.py
@@ -192,12 +192,14 @@
     left = [(b, a) for a, b in right]
     blocks = [block]
     from_left, from_right = block, block
-    for step in range(n // 2):
+    for _ in range(n // 2 - 1):
         from_left = lax.ppermute(from_left, "tensor", right)
-        blocks.append(from_left)
-        if step < n // 2 - 1:
-            from_right = lax.ppermute(from_right, "tensor", left)
-            blocks.append(from_right)
+        from_right = lax.ppermute(from_right, "tensor", left)
+        blocks += [from_left, from_right]
+    half = block.shape[0] // 2
+    upper = lax.ppermute(from_left[:half], "tensor", right)
+    lower = lax.ppermute(from_right[half:], "tensor", left)
+    blocks.append(jnp.concatenate([upper, lower], axis=0))
     return blocks
 
 

time: 381 us -> 383 us (level)
    ppermute x0 -> x2, starting transfers between devices: none -> 4.63 us  [the longest x1 2.48 us: ring_blocks(): upper = lax.ppermute(from_left[:half], 'tensor', right)]
    ppermute x4 -> x3, starting transfers between devices: 34.9 us -> 32.4 us  [ring_blocks(): from_left = lax.ppermute(from_left, 'tensor', right)]
    unnamed x31 -> x30, local copies, waits for them, and re-layouts: 26 us -> 23.7 us
    ppermute x4 -> x3, waiting for transfers between devices: 62 us -> 59.9 us  [ring_blocks(): from_left = lax.ppermute(from_left, 'tensor', right)]
  transfers between devices with their start and end apart: 11 -> 12, of which waited for: 5 -> 4; matrix products, arithmetic and copies ran while one was open for 24% -> 25% of each run, Pallas kernels for 26% -> 25%
where the time goes in v1:
time: 383 us; the launch traced here: 380 us
  Pallas kernels  96.8 us (25%)
  waiting for transfers between devices  61.6 us (16%)
  local copies, waits for them, and re-layouts  60.1 us (16%)
  matrix products  55 us (14%)
  starting transfers between devices  43.1 us (11%)
  blocking collectives  37.1 us (10%)
  between operations  15.4 us (4%)
  other arithmetic  11.1 us (3%)
    pallas_call x1, Pallas kernels, exchange(): pl.pallas_call(lambda *refs: exchange_kernel(n, *refs), out_shape=(jax.Sh...  91.7 us
    ppermute x3, waiting for transfers between devices, ring_blocks(): from_left = lax.ppermute(from_left, 'tensor', right)  59.9 us
    ppermute x3, starting transfers between devices, ring_blocks(): from_left = lax.ppermute(from_left, 'tensor', right)  32.4 us
    all_to_all x1, blocking collectives, to_features(): lax.all_to_all(block.reshape(count, pp, width), ('frame', 'tensor'), 0, 0...  31.9 us
    unnamed x30, local copies, waits for them, and re-layouts  23.7 us
    dot_general x6, matrix products, bdot(): return jnp.dot(a, b, preferred_element_type=jnp.float32)  19.7 us
    sub x1, matrix products, spatial_attention(): weights = jax.nn.softmax(scores, axis=-1).astype(jnp.bfloat16)  15.1 us
    dot_general x1, matrix products, spatial_attention(): jnp.einsum('hpq,hdq->phd', weights, projected[:, 2], preferred_element_ty...  12.1 us
  transfers between devices with their start and end apart: 12, of which 4 were waited for; matrix products, arithmetic and copies ran while one was open for 25% of the time, Pallas kernels for 25%

profile of v1, /device:TPU:0, one launch (start us, length us, event | category | flops | bytes accessed | tf_op | source)
XLA Modules:
  0.0 380.2 jit_solution(3297415787189569496)
XLA Ops:
  20.1 91.7 %exchange.1 = (bf16[8,144,1920]{2,1,0:T(8,128)(2,1)S(1)}, f32[8,88,128]{2,1,0:T(8,128)S(1)}) custom-call(bf16[144,1920]{1,0:T(8,128)(2,1)S(1)} %bitcast.114, f32[88,128]{1,0:T(8,128)S(1)} %pad.30.refs_1_), custom_call_target="tpu_custom_call" | custom-call | bytes 100000000 | tf_op jit(solution)/shard_map/exchange/pallas_call | solution.py:125
  121.9 3.1 convert_reduce_fusion
  126.8 4.0 %fusion.33 = bf16[1920,432]{0,1:T(8,128)(2,1)} fusion(bf16[1152,432]{0,1:T(8,128)(2,1)S(1)} %copy-done.7, bf16[1152,1920]{1,0:T(8,128)(2,1)S(1)} %bitcast.113, f32[1152]{0:T(1024)S(1)} %get-tuple-element.45, f32[1152]{0:T(1024)S(1)} %get-tuple-element.46, f32[1920]{0:T(1024)S(1)} %add_rsqrt_fusion, f32[1920]{0:T(1024)S(1)} %broadcast_multiply_fusion), kind=kOutput, calls=%fused_computation.36 | convolution fusion | flops 1925130240 | bytes 7102464 | tf_op jit(solution)/shard_map/kn,kp->np/dot_general | solution.py:150
  130.8 15.1 %fusion.81 = (f32[2,1920]{1,0:T(2,128)S(1)}, f32[2,1920,1920]{1,2,0:T(8,128)}) fusion(bf16[2,3,72,1920]{3,2,1,0:T(8,128)(2,1)} %bitcast.131), kind=kOutput, calls=%fused_computation.144 | convolution fusion | flops 1083803520 | bytes 30612480 | tf_op jit(solution)/shard_map/sub | solution.py:157
  145.9 12.1 %fusion.49 = bf16[1920,2,72]{0,2,1:T(8,128)(2,1)S(1)} fusion(f32[2,1920,1920]{1,2,0:T(8,128)} %get-tuple-element.52, f32[2,1920]{1,0:T(2,128)S(1)} %get-tuple-element.51, bf16[2,3,72,1920]{3,2,1,0:T(8,128)(2,1)} %bitcast.132), kind=kOutput, calls=%fused_computation.54 | convolution fusion | flops 1076705280 | bytes 30612480 | tf_op jit(solution)/shard_map/hpq,hdq->phd/dot_general | solution.py:158
  163.4 4.0 %all-to-all-start = ((bf16[32,64,336]{2,1,0:T(8,128)(2,1)}), bf16[32,64,336]{2,1,0:T(8,128)(2,1)S(1)}, u32[]{:S(2)}, u32[]{:S(2)}) async-start(bf16[32,64,336]{2,1,0:T(8,128)(2,1)} %bitcast.117), calls=%async_computation | async-start | bytes 3145728 | tf_op jit(solution)/shard_map/all_to_all | solution.py:314
  167.5 5.2 %all-reduce.8 = s32[4]{0:T(128)S(1)} all-reduce(s32[4]{0:T(128)S(1)} %dynamic-update-slice), channel_id=1, replica_groups=mesh['frame'=4,'tensor'=8] {'frame'}, use_global_device_ids=true, to_apply=%add.8 | all-reduce | flops 4 | bytes 32
  172.7 4.3 %collective-permute-done.1 = bf16[576,1152]{1,0:T(8,128)(2,1)} collective-permute-done((bf16[576,1152]{1,0:T(8,128)(2,1)}, bf16[576,1152]{1,0:T(8,128)(2,1)}, u32[]{:S(2)}, u32[]{:S(2)}) %collective-permute-start.1) | collective-permute-done | bytes 1327136 | tf_op jit(solution)/shard_map/ppermute | solution.py:196
  177.0 21.4 %collective-permute-start.3 = (bf16[576,1152]{1,0:T(8,128)(2,1)}, bf16[576,1152]{1,0:T(8,128)(2,1)}, u32[]{:S(2)}, u32[]{:S(2)}) collective-permute-start(bf16[576,1152]{1,0:T(8,128)(2,1)} %collective-permute-done.1), channel_id=1, source_target_pairs={{0,2},{2,4},{4,6},{6,7},{7,5},{5,3},{3,1},{1,0},{8,10},{10,12},{12... | collective-permute-start | bytes 3981320 | tf_op jit(solution)/shard_map/ppermute | solution.py:196
  198.8 2.4 slice_dynamic-update-slice_fusion.9
  201.3 2.5 slice_dynamic-update-slice_fusion.8
  203.7 39.7 %collective-permute-done.3 = bf16[576,1152]{1,0:T(8,128)(2,1)} collective-permute-done((bf16[576,1152]{1,0:T(8,128)(2,1)}, bf16[576,1152]{1,0:T(8,128)(2,1)}, u32[]{:S(2)}, u32[]{:S(2)}) %collective-permute-start.3) | collective-permute-done | bytes 1327136 | tf_op jit(solution)/shard_map/ppermute | solution.py:196
  243.4 9.9 %collective-permute-start.5 = (bf16[576,1152]{1,0:T(8,128)(2,1)}, bf16[576,1152]{1,0:T(8,128)(2,1)}, u32[]{:S(2)}, u32[]{:S(2)}) collective-permute-start(bf16[576,1152]{1,0:T(8,128)(2,1)} %collective-permute-done.3), channel_id=1, source_target_pairs={{0,2},{2,4},{4,6},{6,7},{7,5},{5,3},{3,1},{1,0},{8,10},{10,12},{12... | collective-permute-start | bytes 3981320 | tf_op jit(solution)/shard_map/ppermute | solution.py:196
  253.3 2.5 slice_dynamic-update-slice_fusion.7
  255.8 2.5 slice_dynamic-update-slice_fusion.6
  265.6 16.0 %collective-permute-done.5 = bf16[576,1152]{1,0:T(8,128)(2,1)} collective-permute-done((bf16[576,1152]{1,0:T(8,128)(2,1)}, bf16[576,1152]{1,0:T(8,128)(2,1)}, u32[]{:S(2)}, u32[]{:S(2)}) %collective-permute-start.5) | collective-permute-done | bytes 1327136 | tf_op jit(solution)/shard_map/ppermute | solution.py:196
  281.6 2.6 fusion.80
  284.2 2.5 collective-permute-start.7
  286.7 2.7 slice_dynamic-update-slice_fusion.5
  291.5 8.9 %fusion.79 = (bf16[32,48,1152]{2,1,0:T(8,128)(2,1)S(1)}, bf16[32,48,1152]{2,1,0:T(8,128)(2,1)S(1)}, bf16[32,48,1152]{2,1,0:T(8,128)(2,1)S(1)}, bf16[32,48,1152]{2,1,0:T(8,128)(2,1)S(1)}, bf16[32,48,1152]{2,1,0:T(8,128)(2,1)}) fusion(bf16[32,240,1152]{2,1,0:T(8,128)(2,1)} %all-gather.2.cloned.1.call-done), kind=kLoop, calls=%fused_computation.142 | loop fusion | bytes 35389440 | tf_op jit(solution)/shard_map/slice | solution.py:298
  300.4 3.3 fusion.82
  308.0 5.1 %temporal.1 = bf16[256,1536]{1,0:T(8,128)(2,1)S(1)} custom-call(bf16[256,1536]{1,0:T(8,128)(2,1)S(1)} %convolution_convert_fusion.2.refs_0_, bf16[256,1536]{1,0:T(8,128)(2,1)S(1)} %convolution_convert_fusion.1.refs_1_, bf16[256,1536]{1,0:T(8,128)(2,1)S(1)} %convolution_convert_fusion.refs_2_, f32[4,1536]{1,0:T(4,128)S(1)} %tile.9.refs_3_, ...), custom_call_target="tpu_custom_call" | custom-call | tf_op jit(solution)/shard_map/temporal/pallas_call | solution.py:263
  319.0 12.2 %fusion.43 = f32[512,1152]{1,0:T(8,128)} fusion(bf16[2304,1152]{1,0:T(8,128)(2,1)} %constant_dynamic-update-slice_fusion.3, bf16[2304,1152]{1,0:T(8,128)(2,1)} %constant_dynamic-update-slice_fusion, bf16[256,1152]{1,0:T(8,128)(2,1)S(1)} %collective-permute-done, bf16[256,1152]{1,0:T(8,128)(2,1)S(1)} %add_convert_fusion), kind=kOutput, calls=%fused_computation.49 | convolution fusion | flops 5448794112 | bytes 14155776 | tf_op jit(solution)/shard_map/dot_general | solution.py:33
  337.9 31.9 %all_to_all.10 = bf16[32,64,144]{2,1,0:T(8,128)(2,1)S(1)} all-to-all(bf16[32,64,144]{2,1,0:T(8,128)(2,1)S(1)} %bitcast.120), channel_id=1, replica_groups=mesh['frame'=4,'tensor'=8] {'frame','tensor'}, dimensions={0} | all-to-all | bytes 1179648 | tf_op jit(solution)/shard_map/all_to_all | solution.py:319
  (105 shorter events, 59.3 us)
Async XLA Ops:
  6.5 13.1 %copy-start = (bf16[144,10368]{1,0:T(8,128)(2,1)S(1)}, bf16[144,10368]{1,0:T(8,128)(2,1)}, u32[]{:S(2)}) copy-start(bf16[144,10368]{1,0:T(8,128)(2,1)} %param.17) | copy-start | bytes 8957956
  6.5 285.0 %all-gather.2.cloned.1.call-start = ((), (), s32[]{:S(2)}) async-start(), calls=%async_computation.2 | async-start | bytes 18247680 | tf_op jit(solution)/shard_map/all_gather | solution.py:179
  14.0 1.4 copy-start.5
  16.2 3.9 %copy-start.4 = (bf16[1920,144]{0,1:T(8,128)(2,1)S(1)}, bf16[1920,144]{0,1:T(8,128)(2,1)}, u32[]{:S(2)}) copy-start(bf16[1920,144]{0,1:T(8,128)(2,1)} %param.12) | copy-start | bytes 1658884
  111.8 2.0 copy-start.2
  119.4 57.6 %collective-permute-start.1 = (bf16[576,1152]{1,0:T(8,128)(2,1)}, bf16[576,1152]{1,0:T(8,128)(2,1)}, u32[]{:S(2)}, u32[]{:S(2)}) collective-permute-start(bf16[576,1152]{1,0:T(8,128)(2,1)} %pad_maximum_fusion), channel_id=1, source_target_pairs={{0,2},{2,4},{4,6},{6,7},{7,5},{5,3},{3,1},{1,0},{8,10},{10,12},{12... | collective-permute-start | bytes 3981320 | tf_op jit(solution)/shard_map/ppermute | solution.py:196
  120.5 77.9 %collective-permute-start.2 = (bf16[576,1152]{1,0:T(8,128)(2,1)}, bf16[576,1152]{1,0:T(8,128)(2,1)}, u32[]{:S(2)}, u32[]{:S(2)}) collective-permute-start(bf16[576,1152]{1,0:T(8,128)(2,1)} %pad_maximum_fusion), channel_id=1, source_target_pairs={{2,0},{4,2},{6,4},{7,6},{5,7},{3,5},{1,3},{0,1},{10,8},{12,10},{14... | collective-permute-start | bytes 3981320 | tf_op jit(solution)/shard_map/ppermute | solution.py:197
  121.9 3.6 copy-start.3
  125.0 1.7 copy-start.7
  158.0 2.1 copy-start.8
  163.4 94.8 %all-to-all-start = ((bf16[32,64,336]{2,1,0:T(8,128)(2,1)}), bf16[32,64,336]{2,1,0:T(8,128)(2,1)S(1)}, u32[]{:S(2)}, u32[]{:S(2)}) async-start(bf16[32,64,336]{2,1,0:T(8,128)(2,1)} %bitcast.117), calls=%async_computation | async-start | bytes 3145728 | tf_op jit(solution)/shard_map/all_to_all | solution.py:314
  177.0 66.4 %collective-permute-start.3 = (bf16[576,1152]{1,0:T(8,128)(2,1)}, bf16[576,1152]{1,0:T(8,128)(2,1)}, u32[]{:S(2)}, u32[]{:S(2)}) collective-permute-start(bf16[576,1152]{1,0:T(8,128)(2,1)} %collective-permute-done.1), channel_id=1, source_target_pairs={{0,2},{2,4},{4,6},{6,7},{7,5},{5,3},{3,1},{1,0},{8,10},{10,12},{12... | collective-permute-start | bytes 3981320 | tf_op jit(solution)/shard_map/ppermute | solution.py:196
  198.4 54.9 %collective-permute-start.4 = (bf16[576,1152]{1,0:T(8,128)(2,1)}, bf16[576,1152]{1,0:T(8,128)(2,1)}, u32[]{:S(2)}, u32[]{:S(2)}) collective-permute-start(bf16[576,1152]{1,0:T(8,128)(2,1)} %collective-permute-done.2), channel_id=1, source_target_pairs={{2,0},{4,2},{6,4},{7,6},{5,7},{3,5},{1,3},{0,1},{10,8},{12,10},{14... | collective-permute-start | bytes 3981320 | tf_op jit(solution)/shard_map/ppermute | solution.py:197
  243.4 38.2 %collective-permute-start.5 = (bf16[576,1152]{1,0:T(8,128)(2,1)}, bf16[576,1152]{1,0:T(8,128)(2,1)}, u32[]{:S(2)}, u32[]{:S(2)}) collective-permute-start(bf16[576,1152]{1,0:T(8,128)(2,1)} %collective-permute-done.3), channel_id=1, source_target_pairs={{0,2},{2,4},{4,6},{6,7},{7,5},{5,3},{3,1},{1,0},{8,10},{10,12},{12... | collective-permute-start | bytes 3981320 | tf_op jit(solution)/shard_map/ppermute | solution.py:196
  253.3 33.4 %collective-permute-start.6 = (bf16[576,1152]{1,0:T(8,128)(2,1)}, bf16[576,1152]{1,0:T(8,128)(2,1)}, u32[]{:S(2)}, u32[]{:S(2)}) collective-permute-start(bf16[576,1152]{1,0:T(8,128)(2,1)} %collective-permute-done.4), channel_id=1, source_target_pairs={{2,0},{4,2},{6,4},{7,6},{5,7},{3,5},{1,3},{0,1},{10,8},{12,10},{14... | collective-permute-start | bytes 3981320 | tf_op jit(solution)/shard_map/ppermute | solution.py:197
  284.2 30.9 %collective-permute-start.7 = (bf16[288,1152]{1,0:T(8,128)(2,1)}, bf16[288,1152]{1,0:T(8,128)(2,1)}, u32[]{:S(2)}, u32[]{:S(2)}) collective-permute-start(bf16[288,1152]{1,0:T(8,128)(2,1)} %get-tuple-element.24), channel_id=1, source_target_pairs={{0,2},{2,4},{4,6},{6,7},{7,5},{5,3},{3,1},{1,0},{8,10},{10,12},{12... | collective-permute-start | bytes 1990664 | tf_op jit(solution)/shard_map/ppermute | solution.py:200
  289.4 11.0 %copy-start.6 = (f32[256,1152]{1,0:T(8,128)S(1)}, f32[256,1152]{1,0:T(8,128)}, u32[]{:S(2)}) copy-start(f32[256,1152]{1,0:T(8,128)} %reshape.208) | copy-start | bytes 3538948
  289.4 27.7 %collective-permute-start.8 = (bf16[288,1152]{1,0:T(8,128)(2,1)}, bf16[288,1152]{1,0:T(8,128)(2,1)}, u32[]{:S(2)}, u32[]{:S(2)}) collective-permute-start(bf16[288,1152]{1,0:T(8,128)(2,1)} %get-tuple-element.29), channel_id=1, source_target_pairs={{2,0},{4,2},{6,4},{7,6},{5,7},{3,5},{1,3},{0,1},{10,8},{12,10},{14... | collective-permute-start | bytes 1990664 | tf_op jit(solution)/shard_map/ppermute | solution.py:201
  315.0 4.1 %collective-permute-start = (bf16[256,1152]{1,0:T(8,128)(2,1)S(1)}, bf16[256,1152]{1,0:T(8,128)(2,1)S(1)}, u32[]{:S(2)}, u32[]{:S(2)}) collective-permute-start(bf16[256,1152]{1,0:T(8,128)(2,1)S(1)} %add_convert_fusion), channel_id=1, source_target_pairs={{0,8},{8,0},{16,24},{24,16},{1,9},{9,1},{17,25},{25,17},{2,10},{10... | collective-permute-start | bytes 1769480 | tf_op jit(solution)/shard_map/ppermute | solution.py:350
  332.6 2.2 collective-permute-start.9
  337.9 35.2 %copy-start.1 = (bf16[144,10368]{1,0:T(8,128)(2,1)S(1)}, bf16[144,10368]{1,0:T(8,128)(2,1)}, u32[]{:S(2)}) copy-start(bf16[144,10368]{1,0:T(8,128)(2,1)} %param.17) | copy-start | bytes 8957956
Sparse Core Ops, SparseCore 0:
  16.4 190.3 all-gather.1
